TPU v7x, 768 devices: a whole 4x8x12 slice. The times are simulated.
768 devices in a mesh: ctx: 96 (over y_hi, z, core), tp: 8 (over x, y_lo).
Axes of the slice: x: 4, y: 8 (y_hi: 4, y_lo: 2; y = y_hi * 2 + y_lo), z: 12, core: 2. Of those that a mesh axis runs over, the one named last changes fastest.
Arguments:
- queries: bfloat16 [49152, 4096], P('ctx', 'tp'), may hold values from -140 to 140
- key_vecs: bfloat16 [49152, 1024], P('ctx', 'tp'), may hold values from -6 to 6
- value_vecs: bfloat16 [49152, 1024], P('ctx', 'tp'), may hold values from -6 to 6
- out_grad: bfloat16 [49152, 4096], P('ctx', 'tp'), may hold values from -6 to 6
- doc_ids: int32 [384], replicated, may hold values from 0 to 127, never falling along the last dimension, each value on 1 to 8 neighbouring positions
Outputs:
- attended: bfloat16 [49152, 4096], P('ctx', 'tp')
- query_grad: bfloat16 [49152, 4096], P('ctx', 'tp')
- key_grad: bfloat16 [49152, 1024], P('ctx', 'tp')
- value_grad: bfloat16 [49152, 1024], P('ctx', 'tp')
Inputs may be any that keep to these rules, and one draw needn't show every extreme that they name: doc_ids never fall along the sequence; each document covers 1 to 8 blocks and one covers exactly 8.
All inputs are finite; a program needn't handle non-finite values.
Results may differ from a plain program's by a relative error of at most 0.0075.
Values may be sent and summed in bfloat16 or wider, within the bound.
A program may use at most 64 MiB of HBM per device.

v0:
```python
import jax
import jax.numpy as jnp
from jax import lax
from jax.sharding import PartitionSpec as P

QH = 32
KVH = 8
HD = 128
BLK = 128
REACH = 2


negative_fill = -1e30


def from_behind(block, axis, distance):
    devices = range(lax.axis_size(axis))
    route = [(i - distance, i) for i in devices if i - distance in devices]
    return lax.ppermute(block, axis, route)


def body(queries, key_vecs, value_vecs, out_grad, doc_ids):
    length_dev = queries.shape[0]
    kv_heads = key_vecs.shape[1] // HD
    group_size = QH // KVH
    scale_factor = HD ** (-0.5)
    blocks_dev = length_dev // BLK
    ctx_index = lax.axis_index("ctx")
    query_split = queries.reshape(length_dev, kv_heads, group_size, HD)
    grad_split = out_grad.reshape(length_dev, kv_heads, group_size, HD)
    own_pair = jnp.stack([key_vecs, value_vecs])
    windows = [own_pair]
    for offset in range(1, REACH + 1):
        windows.append(from_behind(own_pair, "ctx", offset))
    docs_pad = jnp.concatenate([jnp.full((REACH * blocks_dev,), -1, jnp.int32), doc_ids])
    query_docs = jnp.repeat(
        lax.dynamic_slice_in_dim(doc_ids, ctx_index * blocks_dev, blocks_dev, 0), BLK
    )
    query_pos = ctx_index * length_dev + jnp.arange(length_dev, dtype=jnp.int32)
    masks = []
    lives = []
    scores = []
    for offset in range(REACH + 1):
        key_docs = jnp.repeat(
            lax.dynamic_slice_in_dim(
                docs_pad, (ctx_index - offset + REACH) * blocks_dev, blocks_dev, 0
            ),
            BLK,
        )
        key_pos = (ctx_index - offset) * length_dev + jnp.arange(length_dev, dtype=jnp.int32)
        allowed = (
            (query_docs[:, None] == key_docs[None, :])
            & (key_pos[None, :] <= query_pos[:, None])
            & (key_pos[None, :] >= 0)
        )
        live = jnp.any(allowed)
        key_split = windows[offset][0].reshape(length_dev, kv_heads, HD)

        def score_fn(key_split=key_split):
            return (
                jnp.einsum(
                    "qhgd,khd->hgqk", query_split, key_split, preferred_element_type=jnp.float32
                )
                * scale_factor
            )

        if offset == 0:
            scores.append(score_fn())
        else:
            scores.append(score_fn())
        masks.append(allowed)
        lives.append(live)
    highest = jnp.max(
        jnp.stack(
            [
                jnp.max(jnp.where(masks[o], scores[o], negative_fill), axis=-1)
                for o in range(REACH + 1)
            ]
        ),
        axis=0,
    )[..., None]
    total = sum(
        (
            jnp.sum(jnp.where(masks[o], jnp.exp(scores[o] - highest), 0.0), axis=-1, keepdims=True)
            for o in range(REACH + 1)
        )
    )
    lse = highest + jnp.log(total)
    probs = [jnp.where(masks[o], jnp.exp(scores[o] - lse), 0.0) for o in range(REACH + 1)]
    probs16 = [piece_p.astype(jnp.bfloat16) for piece_p in probs]
    out_blank = jnp.zeros((length_dev, kv_heads, group_size, HD), jnp.float32)
    output = out_blank
    for offset in range(REACH + 1):
        value_split = windows[offset][1].reshape(length_dev, kv_heads, HD)

        def apply_fn(offset=offset, value_split=value_split):
            return jnp.einsum(
                "hgqk,khd->qhgd", probs16[offset], value_split, preferred_element_type=jnp.float32
            )

        if offset == 0:
            output = apply_fn()
        else:
            output = output + apply_fn()
    output16 = output.astype(jnp.bfloat16)
    delta = jnp.sum(grad_split.astype(jnp.float32) * output16.astype(jnp.float32), axis=-1)
    delta_hgq = jnp.transpose(delta, (1, 2, 0))[..., None]
    query_acc = out_blank
    partials = []
    for offset in range(REACH + 1):
        key_split = windows[offset][0].reshape(length_dev, kv_heads, HD)
        value_split = windows[offset][1].reshape(length_dev, kv_heads, HD)

        def back_fn(offset=offset, key_split=key_split, value_split=value_split):
            dprobs = jnp.einsum(
                "qhgd,khd->hgqk", grad_split, value_split, preferred_element_type=jnp.float32
            )
            dscores = (probs[offset] * (dprobs - delta_hgq)).astype(jnp.bfloat16)
            query_term = (
                jnp.einsum("hgqk,khd->qhgd", dscores, key_split, preferred_element_type=jnp.float32)
                * scale_factor
            )
            key_term = (
                jnp.einsum(
                    "hgqk,qhgd->khd", dscores, query_split, preferred_element_type=jnp.float32
                )
                * scale_factor
            )
            value_term = jnp.einsum(
                "hgqk,qhgd->khd", probs16[offset], grad_split, preferred_element_type=jnp.float32
            )
            stacked = jnp.stack(
                [
                    key_term.reshape(length_dev, kv_heads * HD),
                    value_term.reshape(length_dev, kv_heads * HD),
                ]
            )
            return (query_term, stacked)

        if offset == 0:
            query_term, stacked = back_fn()
        else:
            query_term, stacked = back_fn()
        query_acc = query_acc + query_term
        partials.append(stacked)
    returned = jnp.zeros_like(partials[0])
    for offset in range(REACH, 0, -1):
        returned = from_behind(returned + partials[offset], "ctx", -1)
    summed = partials[0] + returned
    attended = output16.reshape(length_dev, kv_heads * group_size * HD)
    query_grad = query_acc.astype(jnp.bfloat16).reshape(length_dev, kv_heads * group_size * HD)
    key_grad = summed[0].astype(jnp.bfloat16)
    value_grad = summed[1].astype(jnp.bfloat16)
    return (attended, query_grad, key_grad, value_grad)


def solution(mesh):
    placed = (P("ctx", "tp"), P("ctx", "tp"), P("ctx", "tp"), P("ctx", "tp"), P())
    return jax.shard_map(
        body,
        mesh=mesh,
        in_specs=placed,
        out_specs=(P("ctx", "tp"), P("ctx", "tp"), P("ctx", "tp"), P("ctx", "tp")),
        check_vma=False,
    )
```

profile of v0, /device:TPU:50, one launch (start us, length us, event | category | flops | bytes accessed | tf_op | source)
XLA Modules:
  0.0 77.6 jit_solution(1862088279559024331)
XLA Ops:
  0.6 0.0 copy-start
  0.6 1.1 %pad_maximum_fusion.1 = bf16[2,512,128]{2,1,0:T(8,128)(2,1)S(1)} fusion(bf16[1,512,128]{2,1,0:T(8,128)(2,1)} %bitcast.394, bf16[1,512,128]{2,1,0:T(8,128)(2,1)} %bitcast.393), kind=kLoop, calls=%fused_computation.100 | loop fusion | flops 131072 | bytes 524288 | tf_op jit(solution)/shard_map/stack | solution.py:31
  1.7 4.3 %collective-permute-start.1 = (bf16[2,512,128]{2,1,0:T(8,128)(2,1)S(1)}, bf16[2,512,128]{2,1,0:T(8,128)(2,1)S(1)}, u32[]{:S(2)}, u32[]{:S(2)}) collective-permute-start(bf16[2,512,128]{2,1,0:T(8,128)(2,1)S(1)} %pad_maximum_fusion.1), channel_id=1, source_target_pairs={{0,16},{8,24},{16,32},{24,40},{32,48},{40,56},{48,64},{56,72},{64,... | collective-permute-start | bytes 786440 | tf_op jit(solution)/shard_map/ppermute | solution.py:19
  6.0 1.9 %collective-permute-start = (bf16[2,512,128]{2,1,0:T(8,128)(2,1)S(1)}, bf16[2,512,128]{2,1,0:T(8,128)(2,1)S(1)}, u32[]{:S(2)}, u32[]{:S(2)}) collective-permute-start(bf16[2,512,128]{2,1,0:T(8,128)(2,1)S(1)} %pad_maximum_fusion.1), channel_id=1, source_target_pairs={{0,8},{8,16},{16,24},{24,32},{32,40},{40,48},{48,56},{56,64},{64,7... | collective-permute-start | bytes 786440 | tf_op jit(solution)/shard_map/ppermute | solution.py:19
  8.0 1.3 %copy.19 = f32[512,512]{0,1:T(8,128)S(1)} copy(bf16[512,512]{1,0:T(8,128)(2,1)} %param.8) | data formatting | bytes 1572864 | tf_op jit(solution)/shard_map/convert_element_type | solution.py:106
  9.3 0.9 %pad_dynamic-slice_fusion.1 = (s32[4]{0:T(128)S(1)}, s32[4]{0:T(128)S(1)}, s32[4]{0:T(128)S(1)}, s32[4]{0:T(128)S(1)}) fusion(s32[]{:T(128)S(6)} %select_n.43, s32[384]{0:T(512)} %param.9, s32[]{:T(128)S(6)} %select_n.45, s32[]{:T(128)S(6)} %select_n.41, s32[]{:T(128)S(6)} %select_n.40), kind=kLoop, calls=%fused_computation.130 | loop fusion | bytes 2640 | tf_op jit(solution)/shard_map/dynamic_slice | solution.py:45
  10.2 0.1 broadcast_bitcast_fusion
  10.3 0.1 broadcast_bitcast_fusion.2
  10.3 1.1 %and_and_fusion.1 = (pred[512,512]{0,1:T(8,128)(4,1)S(1)}, pred[512,512]{0,1:T(8,128)(4,1)S(1)}, pred[512,512]{0,1:T(8,128)(4,1)S(1)}) fusion(s32[512]{0:T(512)S(1)} %iota_add_fusion.2, s32[512]{0:T(512)S(1)} %get-tuple-element.31, s32[512]{0:T(512)S(1)} %get-tuple-element.33, s32[512]{0:T(512)S(1)} %get-tuple-element.29, ...), kind=kLoop, calls=%fused_computation.79 | loop fusion | flops 3145728 | bytes 802304 | tf_op jit(solution)/shard_map/and | solution.py:52
  11.4 0.0 copy-done
  11.4 1.8 %fusion.18 = (f32[4,512]{1,0:T(4,128)S(1)}, f32[512,512,4]{1,0,2:T(8,128)S(1)}) fusion(pred[512,512]{0,1:T(8,128)(4,1)S(1)} %get-tuple-element.15, bf16[512,128]{1,0:T(8,128)(2,1)} %param.6, bf16[512,512]{1,0:T(8,128)(2,1)S(1)} %copy-done), kind=kOutput, calls=%fused_computation.30 | convolution fusion | flops 271579136 | bytes 5120000 | tf_op jit(solution)/shard_map/qhgd,khd->hgqk/dot_general | solution.py:61
  13.2 0.0 copy-start.1
  13.2 18.8 %collective-permute-done.1 = bf16[2,512,128]{2,1,0:T(8,128)(2,1)S(1)} collective-permute-done((bf16[2,512,128]{2,1,0:T(8,128)(2,1)S(1)}, bf16[2,512,128]{2,1,0:T(8,128)(2,1)S(1)}, u32[]{:S(2)}, u32[]{:S(2)}) %collective-permute-start.1) | collective-permute-done | bytes 262176 | tf_op jit(solution)/shard_map/ppermute | solution.py:19
  32.1 0.9 %fusion.6 = (f32[4,512]{1,0:T(4,128)S(1)}, f32[512,512,4]{1,0,2:T(8,128)S(1)}) fusion(pred[512,512]{0,1:T(8,128)(4,1)S(1)} %get-tuple-element.14, bf16[2,512,128]{2,1,0:T(8,128)(2,1)S(1)} %collective-permute-done.1, bf16[512,512]{1,0:T(8,128)(2,1)S(1)} %copy-done), kind=kOutput, calls=%fused_computation.12 | convolution fusion | flops 271579136 | bytes 5120000 | tf_op jit(solution)/shard_map/qhgd,khd->hgqk/dot_general | solution.py:61
  33.0 2.0 %collective-permute-done = bf16[2,512,128]{2,1,0:T(8,128)(2,1)S(1)} collective-permute-done((bf16[2,512,128]{2,1,0:T(8,128)(2,1)S(1)}, bf16[2,512,128]{2,1,0:T(8,128)(2,1)S(1)}, u32[]{:S(2)}, u32[]{:S(2)}) %collective-permute-start) | collective-permute-done | bytes 262176 | tf_op jit(solution)/shard_map/ppermute | solution.py:19
  34.9 0.9 %fusion.12 = (f32[4,512]{1,0:T(4,128)S(1)}, f32[512,512,4]{1,0,2:T(8,128)S(1)}) fusion(pred[512,512]{0,1:T(8,128)(4,1)S(1)} %get-tuple-element.13, bf16[2,512,128]{2,1,0:T(8,128)(2,1)S(1)} %collective-permute-done, bf16[512,512]{1,0:T(8,128)(2,1)S(1)} %copy-done), kind=kOutput, calls=%fused_computation.21 | convolution fusion | flops 271579136 | bytes 5120000 | tf_op jit(solution)/shard_map/qhgd,khd->hgqk/dot_general | solution.py:61
  35.8 0.0 copy-start.5
  35.8 2.7 %fusion.15 = (f32[4,512]{1,0:T(4,128)S(1)}, f32[4,512]{1,0:T(4,128)S(1)}, f32[4,512]{1,0:T(4,128)S(1)}) fusion(f32[512,512,4]{1,0,2:T(8,128)S(1)} %get-tuple-element.25, f32[4,512]{1,0:T(4,128)S(1)} %maximum_maximum_fusion, pred[512,512]{0,1:T(8,128)(4,1)S(1)} %get-tuple-element.13, f32[512,512,4]{1,0,2:T(8,128)S(1)} %get-tuple-element.21, ...), kind=kLoop, calls=%fused_computation.24 | loop fusion | flops 12576768 | bytes 13402112 | tf_op jit(solution)/shard_map/reduce_sum | solution.py:84
  38.6 0.0 copy-start.3
  38.6 0.0 copy-done.5
  38.6 1.0 %convolution_bitcast_fusion = f32[128,4,512]{2,0,1:T(8,128)S(1)} fusion(bf16[512,128]{1,0:T(8,128)(2,1)S(1)} %copy-done.5, f32[512,512,4]{1,0,2:T(8,128)S(1)} %get-tuple-element.23, f32[4,512]{1,0:T(4,128)S(1)} %log_add_fusion, pred[512,512]{0,1:T(8,128)(4,1)S(1)} %get-tuple-element.15), kind=kOutput, calls=%fused_computation.59 | convolution fusion | flops 272629760 | bytes 5644288 | tf_op jit(solution)/shard_map/hgqk,khd->qhgd/dot_general | solution.py:97
  39.6 0.0 copy-done.3
  39.6 0.9 %convolution_bitcast_fusion.2 = f32[1,512,128]{2,1,0:T(8,128)S(1)} fusion(f32[512,512,4]{1,0,2:T(8,128)S(1)} %get-tuple-element.21, f32[4,512]{1,0:T(4,128)S(1)} %log_add_fusion, pred[512,512]{0,1:T(8,128)(4,1)S(1)} %get-tuple-element.14, bf16[512,512]{1,0:T(8,128)(2,1)S(1)} %copy-done.3), kind=kOutput, calls=%fused_computation.69 | convolution fusion | flops 272629760 | bytes 5251072 | tf_op jit(solution)/shard_map/hgqk,qhgd->khd/dot_general | solution.py:129
  40.5 1.0 %fusion.124 = f32[128,4,512]{2,0,1:T(8,128)S(1)} fusion(bf16[2,512,128]{2,1,0:T(8,128)(2,1)S(1)} %collective-permute-done.1, f32[512,512,4]{1,0,2:T(8,128)S(1)} %get-tuple-element.21, f32[4,512]{1,0:T(4,128)S(1)} %log_add_fusion, pred[512,512]{0,1:T(8,128)(4,1)S(1)} %get-tuple-element.14), kind=kOutput, calls=%fused_computation.123 | convolution fusion | flops 272629760 | bytes 5644288 | tf_op jit(solution)/shard_map/hgqk,khd->qhgd/dot_general | solution.py:97
  41.6 1.1 %multiply_reduce_fusion = (f32[512,4]{0,1:T(4,128)S(1)}, bf16[128,4,512]{2,0,1:T(8,128)(2,1)S(1)}) fusion(f32[512,1,4,128]{0,3,2,1:T(8,128)S(1)} %bitcast.390, f32[128,4,512]{2,0,1:T(8,128)S(1)} %fusion.124, f32[128,4,512]{2,0,1:T(8,128)S(1)} %convolution_bitcast_fusion, f32[512,512,4]{1,0,2:T(8,128)S(1)} %get-tuple-element.25, ...), kind=kOutput, calls=%fused_computation.77 | convolution fusion | flops 274200576 | bytes 8273920 | tf_op jit(solution)/shard_map/hgqk,khd->qhgd/dot_general | solution.py:97
  42.6 0.0 copy-done.1
  42.7 1.5 %fusion.5 = bf16[1,4,512,512]{2,3,1,0:T(8,128)(2,1)S(1)} fusion(f32[512,512,4]{1,0,2:T(8,128)S(1)} %get-tuple-element.23, f32[4,512]{1,0:T(4,128)S(1)} %bitcast.395, f32[4,512]{1,0:T(4,128)S(1)} %log_add_fusion, pred[512,512]{0,1:T(8,128)(4,1)S(1)} %get-tuple-element.15, bf16[512,128]{1,0:T(8,128)(2,1)S(1)} %copy-done.5, bf16[512,512]{1,0:T(8,128)(2,1)S(1)} %copy-done.3), kind=kOutput, calls=%fused_computation.8 | convolution fusion | flops 274726912 | bytes 7225344 | tf_op jit(solution)/shard_map/qhgd,khd->hgqk/dot_general | solution.py:115
  44.1 0.0 copy-start.2
  44.1 1.5 %fusion.1 = bf16[1,4,512,512]{2,3,1,0:T(8,128)(2,1)S(1)} fusion(f32[512,512,4]{1,0,2:T(8,128)S(1)} %get-tuple-element.21, f32[4,512]{1,0:T(4,128)S(1)} %bitcast.396, f32[4,512]{1,0:T(4,128)S(1)} %log_add_fusion, pred[512,512]{0,1:T(8,128)(4,1)S(1)} %get-tuple-element.14, bf16[2,512,128]{2,1,0:T(8,128)(2,1)S(1)} %collective-permute-done.1, ...), kind=kOutput, calls=%fused_computation.2 | convolution fusion | flops 274726912 | bytes 7225344 | tf_op jit(solution)/shard_map/qhgd,khd->hgqk/dot_general | solution.py:115
  45.6 0.7 fusion.77
  46.3 2.1 %collective-permute-start.2 = (f32[2,512,128]{2,1,0:T(8,128)S(1)}, f32[2,512,128]{2,1,0:T(8,128)S(1)}, u32[]{:S(2)}, u32[]{:S(2)}) collective-permute-start(f32[2,512,128]{2,1,0:T(8,128)S(1)} %pad_maximum_fusion), channel_id=1, source_target_pairs={{8,0},{16,8},{24,16},{32,24},{40,32},{48,40},{56,48},{64,56},{72,6... | collective-permute-start | bytes 1572872 | tf_op jit(solution)/shard_map/ppermute | solution.py:19
  48.5 0.0 copy-done.2
  48.5 0.5 fusion.45
  49.0 1.5 %fusion.3 = bf16[1,4,512,512]{2,3,1,0:T(8,128)(2,1)S(1)} fusion(f32[512,512,4]{1,0,2:T(8,128)S(1)} %get-tuple-element.25, f32[4,512]{1,0:T(4,128)S(1)} %bitcast.397, f32[4,512]{1,0:T(4,128)S(1)} %log_add_fusion, pred[512,512]{0,1:T(8,128)(4,1)S(1)} %get-tuple-element.13, bf16[2,512,128]{2,1,0:T(8,128)(2,1)S(1)} %collective-permute-done, ...), kind=kOutput, calls=%fused_computation.5 | convolution fusion | flops 274726912 | bytes 7225344 | tf_op jit(solution)/shard_map/qhgd,khd->hgqk/dot_general | solution.py:115
  50.4 0.5 fusion.58
  50.9 0.5 fusion.61
  51.4 0.7 fusion.83
  52.1 0.9 %convolution_bitcast_fusion.1 = f32[1,512,128]{2,1,0:T(8,128)S(1)} fusion(f32[512,512,4]{1,0,2:T(8,128)S(1)} %get-tuple-element.25, f32[4,512]{1,0:T(4,128)S(1)} %log_add_fusion, pred[512,512]{0,1:T(8,128)(4,1)S(1)} %get-tuple-element.13, bf16[512,512]{1,0:T(8,128)(2,1)S(1)} %copy-done.3), kind=kOutput, calls=%fused_computation.68 | convolution fusion | flops 272629760 | bytes 5251072 | tf_op jit(solution)/shard_map/hgqk,qhgd->khd/dot_general | solution.py:129
  53.0 5.2 %collective-permute-done.2 = f32[2,512,128]{2,1,0:T(8,128)S(1)} collective-permute-done((f32[2,512,128]{2,1,0:T(8,128)S(1)}, f32[2,512,128]{2,1,0:T(8,128)S(1)}, u32[]{:S(2)}, u32[]{:S(2)}) %collective-permute-start.2) | collective-permute-done | bytes 524320 | tf_op jit(solution)/shard_map/ppermute | solution.py:19
  58.2 0.1 maximum_add_fusion.1
  58.2 8.8 %collective-permute-start.3 = (f32[2,512,128]{2,1,0:T(8,128)S(1)}, f32[2,512,128]{2,1,0:T(8,128)S(1)}, u32[]{:S(2)}, u32[]{:S(2)}) collective-permute-start(f32[2,512,128]{2,1,0:T(8,128)S(1)} %maximum_add_fusion.1), channel_id=1, source_target_pairs={{8,0},{16,8},{24,16},{32,24},{40,32},{48,40},{56,48},{64,56},{72,6... | collective-permute-start | bytes 1572872 | tf_op jit(solution)/shard_map/ppermute | solution.py:19
  67.0 1.4 %fusion.89 = f32[1,512,128]{2,1,0:T(8,128)} fusion(bf16[1,4,512,512]{2,3,1,0:T(8,128)(2,1)S(1)} %fusion.5, bf16[512,512]{1,0:T(8,128)(2,1)S(1)} %copy-done), kind=kOutput, calls=%fused_computation.76 | convolution fusion | flops 268500992 | bytes 2883584 | tf_op jit(solution)/shard_map/hgqk,qhgd->khd/dot_general | solution.py:124
  68.4 1.0 %copy.35 = bf16[512,512]{1,0:T(8,128)(2,1)} copy(bf16[512,512]{0,1:T(8,128)(2,1)S(1)} %bitcast.392) | data formatting | bytes 1048576
  69.4 0.0 copy-start.4
  69.4 1.0 %copy.34 = bf16[512,512]{1,0:T(8,128)(2,1)} copy(bf16[512,512]{0,1:T(8,128)(2,1)S(1)} %bitcast.391) | data formatting | bytes 1048576
  70.4 3.1 %convolution_bitcast_fusion.3 = f32[1,512,128]{2,1,0:T(8,128)S(1)} fusion(f32[512,512,4]{1,0,2:T(8,128)} %copy-done.1, f32[4,512]{1,0:T(4,128)S(1)} %log_add_fusion, pred[512,512]{0,1:T(8,128)(4,1)S(1)} %get-tuple-element.15, bf16[512,512]{1,0:T(8,128)(2,1)S(1)} %copy-done.3), kind=kOutput, calls=%fused_computation.70 | convolution fusion | flops 272629760 | bytes 5251072 | tf_op jit(solution)/shard_map/hgqk,qhgd->khd/dot_general | solution.py:129
  73.5 3.4 %collective-permute-done.3 = f32[2,512,128]{2,1,0:T(8,128)S(1)} collective-permute-done((f32[2,512,128]{2,1,0:T(8,128)S(1)}, f32[2,512,128]{2,1,0:T(8,128)S(1)}, u32[]{:S(2)}, u32[]{:S(2)}) %collective-permute-start.3) | collective-permute-done | bytes 524320 | tf_op jit(solution)/shard_map/ppermute | solution.py:19
  76.9 0.0 copy-done.4
  76.9 0.1 fusion.107
  76.9 0.7 slice_bitcast_fusion
  (7 shorter events, 0.1 us)
Async XLA Ops:
  0.6 10.8 %copy-start = (bf16[512,512]{1,0:T(8,128)(2,1)S(1)}, bf16[512,512]{1,0:T(8,128)(2,1)}, u32[]{:S(2)}) copy-start(bf16[512,512]{1,0:T(8,128)(2,1)} %param.5) | copy-start | bytes 1572868
  1.7 30.4 %collective-permute-start.1 = (bf16[2,512,128]{2,1,0:T(8,128)(2,1)S(1)}, bf16[2,512,128]{2,1,0:T(8,128)(2,1)S(1)}, u32[]{:S(2)}, u32[]{:S(2)}) collective-permute-start(bf16[2,512,128]{2,1,0:T(8,128)(2,1)S(1)} %pad_maximum_fusion.1), channel_id=1, source_target_pairs={{0,16},{8,24},{16,32},{24,40},{32,48},{40,56},{48,64},{56,72},{64,... | collective-permute-start | bytes 786440 | tf_op jit(solution)/shard_map/ppermute | solution.py:19
  6.0 28.9 %collective-permute-start = (bf16[2,512,128]{2,1,0:T(8,128)(2,1)S(1)}, bf16[2,512,128]{2,1,0:T(8,128)(2,1)S(1)}, u32[]{:S(2)}, u32[]{:S(2)}) collective-permute-start(bf16[2,512,128]{2,1,0:T(8,128)(2,1)S(1)} %pad_maximum_fusion.1), channel_id=1, source_target_pairs={{0,8},{8,16},{16,24},{24,32},{32,40},{40,48},{48,56},{56,64},{64,7... | collective-permute-start | bytes 786440 | tf_op jit(solution)/shard_map/ppermute | solution.py:19
  13.2 29.4 %copy-start.1 = (f32[512,512,4]{1,0,2:T(8,128)}, f32[512,512,4]{1,0,2:T(8,128)S(1)}, u32[]{:S(2)}) copy-start(f32[512,512,4]{1,0,2:T(8,128)S(1)} %get-tuple-element.23) | copy-start | bytes 12582916
  35.8 2.8 %copy-start.5 = (bf16[512,128]{1,0:T(8,128)(2,1)S(1)}, bf16[512,128]{1,0:T(8,128)(2,1)}, u32[]{:S(2)}) copy-start(bf16[512,128]{1,0:T(8,128)(2,1)} %param.7) | copy-start | bytes 393220
  38.6 1.0 %copy-start.3 = (bf16[512,512]{1,0:T(8,128)(2,1)S(1)}, bf16[512,512]{1,0:T(8,128)(2,1)}, u32[]{:S(2)}) copy-start(bf16[512,512]{1,0:T(8,128)(2,1)} %param.8) | copy-start | bytes 1572868
  44.1 4.3 %copy-start.2 = (bf16[512,128]{1,0:T(8,128)(2,1)S(1)}, bf16[512,128]{1,0:T(8,128)(2,1)}, u32[]{:S(2)}) copy-start(bf16[512,128]{1,0:T(8,128)(2,1)} %param.6) | copy-start | bytes 393220
  46.3 11.8 %collective-permute-start.2 = (f32[2,512,128]{2,1,0:T(8,128)S(1)}, f32[2,512,128]{2,1,0:T(8,128)S(1)}, u32[]{:S(2)}, u32[]{:S(2)}) collective-permute-start(f32[2,512,128]{2,1,0:T(8,128)S(1)} %pad_maximum_fusion), channel_id=1, source_target_pairs={{8,0},{16,8},{24,16},{32,24},{40,32},{48,40},{56,48},{64,56},{72,6... | collective-permute-start | bytes 1572872 | tf_op jit(solution)/shard_map/ppermute | solution.py:19
  58.2 18.6 %collective-permute-start.3 = (f32[2,512,128]{2,1,0:T(8,128)S(1)}, f32[2,512,128]{2,1,0:T(8,128)S(1)}, u32[]{:S(2)}, u32[]{:S(2)}) collective-permute-start(f32[2,512,128]{2,1,0:T(8,128)S(1)} %maximum_add_fusion.1), channel_id=1, source_target_pairs={{8,0},{16,8},{24,16},{32,24},{40,32},{48,40},{56,48},{64,56},{72,6... | collective-permute-start | bytes 1572872 | tf_op jit(solution)/shard_map/ppermute | solution.py:19
  69.4 7.5 %copy-start.4 = (f32[1,512,128]{2,1,0:T(8,128)S(1)}, f32[1,512,128]{2,1,0:T(8,128)}, u32[]{:S(2)}) copy-start(f32[1,512,128]{2,1,0:T(8,128)} %fusion.89) | copy-start | bytes 786436
where the time goes:
time: 78.1 us; the launch traced here: 77.6 us
  waiting for transfers between devices  29.4 us (38%)
  matrix products  20.1 us (26%)
  starting transfers between devices  17.1 us (22%)
  local copies, waits for them, and re-layouts  5.1 us (7%)
  other arithmetic  5.09 us (7%)
  between operations  0.96 us (1%)
    ppermute x4, waiting for transfers between devices, from_behind(): return lax.ppermute(block, axis, route)  29.4 us
    ppermute x4, starting transfers between devices, from_behind(): return lax.ppermute(block, axis, route)  17.1 us
    dot_general x3, matrix products, back_fn(): jnp.einsum('hgqk,qhgd->khd', probs16[offset], grad_split, preferred_eleme...  4.8 us
    dot_general x3, matrix products, back_fn(): jnp.einsum('qhgd,khd->hgqk', grad_split, value_split, preferred_element_t...  4.37 us
    dot_general x3, matrix products, score_fn(): jnp.einsum('qhgd,khd->hgqk', query_split, key_split, preferred_element_ty...  3.53 us
    dot_general x3, matrix products, apply_fn(): jnp.einsum('hgqk,khd->qhgd', probs16[offset], value_split, preferred_elem...  3.11 us
    dot_general x3, matrix products, back_fn(): jnp.einsum('hgqk,qhgd->khd', dscores, query_split, preferred_element_type...  2.82 us
    reduce_sum x1, other arithmetic, body(): jnp.sum(jnp.where(masks[o], jnp.exp(scores[o] - highest), 0.0), axis=-1,...  2.75 us
  transfers between devices with their start and end apart: 4, of which 4 were waited for; matrix products, arithmetic and copies ran while one was open for 22% of the time, Pallas kernels for 0%

commit v1 on v0

v1 whole, which is shorter than its diff:
```python
import functools
import math

import jax
import jax.numpy as jnp
from jax import lax
from jax.experimental import pallas as pl
from jax.experimental.pallas import tpu as pltpu
from jax.sharding import PartitionSpec as P

HD = 128
BLK = 128
HEADS = 4
NB = 4
TOK = NB * BLK
WIN = 11
COLS = HEADS * BLK
OWN = 7 * BLK
ONE = 3 * BLK
SCALE = HD**-0.5
SCALE2 = SCALE * math.log2(math.e)
MESH = pl.DeviceIdType.MESH
F32 = jnp.float32
BF16 = jnp.bfloat16


def dot(a, b):
    return jnp.dot(a, b, preferred_element_type=F32)


def kernel(
    n,
    docs, q_hbm, k_hbm, v_hbm, g_hbm,
    att_out, qg_out, kg_out, vg_out,
    q_in, g_in,
    kwin, vwin, k_t, v_t, q_t, g_t, q_s, g_s,
    e_all, p_all, d_all, top, total, alpha, delta,
    dk_own, dv_own, pk, pv, rk1, rk2, rv1, rv2,
    load_sem, send_sem, recv_sem, back_send, back_recv,
):
    s = lax.axis_index("ctx")
    even = lax.rem(s, 2) == 0
    odd = lax.rem(s, 2) == 1
    prev1, prev2, next1, next2 = s >= 1, s >= 2, s + 1 < n, s + 2 < n

    def to(shift):
        return {"ctx": lax.rem(s + shift + n, n)}

    barrier = pltpu.get_barrier_semaphore()

    @pl.when(prev1)
    def _():
        pl.semaphore_signal(barrier, inc=1, device_id=to(-1), device_id_type=MESH)

    @pl.when(prev2 & even)
    def _():
        pl.semaphore_signal(barrier, inc=1, device_id=to(-2), device_id_type=MESH)

    own = pl.ds(OWN, TOK)
    load_q = pltpu.make_async_copy(q_hbm, q_in, load_sem.at[0])
    load_k = pltpu.make_async_copy(k_hbm, kwin.at[own], load_sem.at[1])
    load_v = pltpu.make_async_copy(v_hbm, vwin.at[own], load_sem.at[2])
    load_g = pltpu.make_async_copy(g_hbm, g_in, load_sem.at[3])

    targets = next1.astype(jnp.int32) + (next2 & even).astype(jnp.int32)

    @pl.when(targets > 0)
    def _():
        pl.semaphore_wait(barrier, targets)

    def send(src, dst, i, shift):
        return pltpu.make_async_remote_copy(
            src, dst, send_sem.at[i], recv_sem.at[i], device_id=to(shift), device_id_type=MESH
        )

    tail = pl.ds(BLK, 3 * BLK)
    one, two, one_tail = pl.ds(ONE, TOK), pl.ds(0, 3 * BLK), pl.ds(ONE + BLK, 3 * BLK)
    k1 = send(k_hbm, kwin.at[one], 0, 1)
    v1 = send(v_hbm, vwin.at[one], 2, 1)
    k2 = send(k_hbm.at[tail], kwin.at[two], 1, 2)
    v2 = send(v_hbm.at[tail], vwin.at[two], 3, 2)
    k2_on = send(kwin.at[one_tail], kwin.at[two], 1, 1)
    v2_on = send(vwin.at[one_tail], vwin.at[two], 3, 1)

    @pl.when(next1)
    def _():
        k1.start()

    @pl.when(next2 & even)
    def _():
        k2.start()

    @pl.when(next1)
    def _():
        v1.start()

    @pl.when(next2 & even)
    def _():
        v2.start()

    for load in (load_q, load_k, load_g, load_v):
        load.start()

    @pl.when(jnp.logical_not(prev1))
    def _():
        kwin[one] = jnp.zeros((TOK, HD), BF16)
        vwin[one] = jnp.zeros((TOK, HD), BF16)

    @pl.when(jnp.logical_not(prev2))
    def _():
        kwin[two] = jnp.zeros((3 * BLK, HD), BF16)
        vwin[two] = jnp.zeros((3 * BLK, HD), BF16)

    def cut(i):
        return slice(i * BLK, (i + 1) * BLK)

    def cols(b):
        return slice(b * COLS, (b + 1) * COLS)

    def split(src, stacked, turned):
        for b in range(NB):
            for h in range(HEADS):
                x = src[cut(b), cut(h)]
                at = slice(b * COLS + h * BLK, b * COLS + (h + 1) * BLK)
                stacked[at, :] = x
                turned[:, at] = x.T

    def turn(src, dst, rows):
        dst[:, rows] = src[rows, :].T

    causal = lax.broadcasted_iota(jnp.int32, (BLK, COLS), 0) <= lax.rem(
        lax.broadcasted_iota(jnp.int32, (BLK, COLS), 1), BLK
    )

    def score(w, b):
        x = dot(kwin[cut(w), :], q_t[:, cols(b)])
        if w == b + 7:
            x = jnp.where(causal, x, -1e30)
        m = jnp.max(x, axis=0, keepdims=True)
        e = jnp.exp2((x - m) * SCALE2)
        top[w : w + 1, cols(b)] = m
        total[w : w + 1, cols(b)] = jnp.sum(e, axis=0, keepdims=True)
        e_all[cut(w), cols(b)] = e

    def reach(w):
        return [b for b in range(NB) if b <= w <= b + 7]

    load_q.wait()
    split(q_in, q_s, q_t)
    load_k.wait()
    for w in range(7, 11):
        for b in reach(w):
            score(w, b)
    turn(kwin, k_t, slice(OWN, OWN + TOK))
    load_g.wait()
    split(g_in, g_s, g_t)
    load_v.wait()
    turn(vwin, v_t, slice(OWN, OWN + TOK))

    @pl.when(prev1)
    def _():
        k1.wait_recv()

    @pl.when(prev1 & next1 & even)
    def _():
        k2_on.start()

    for b in range(NB):
        for w in range(3, 7):
            score(w, b)
    turn(kwin, k_t, slice(ONE, ONE + TOK))

    @pl.when(prev2)
    def _():
        k2.wait_recv()

    for w in range(3):
        for b in reach(w):
            score(w, b)
    turn(kwin, k_t, slice(0, 3 * BLK))

    for b in range(NB):
        mine = docs[s * NB + b]
        ws = range(b, b + 8)
        alike = []
        for w in ws:
            at = s * NB + (w - 7)
            alike.append((docs[jnp.maximum(at, 0)] == mine) & (at >= 0))
        tops = [top[w : w + 1, cols(b)] for w in ws]
        high = tops[-1]
        for t, ok in zip(tops[:-1], alike[:-1]):
            high = jnp.maximum(high, jnp.where(ok, t, -1e30))
        alphas = [
            jnp.where(ok, jnp.exp2((t - high) * SCALE2), 0.0) for t, ok in zip(tops, alike)
        ]
        whole = sum(a * total[w : w + 1, cols(b)] for a, w in zip(alphas, ws))
        inverse = 1.0 / whole
        for a, w in zip(alphas, ws):
            alpha[w : w + 1, cols(b)] = a * inverse

    def prob(w, b):
        p_all[cut(w), cols(b)] = (e_all[cut(w), cols(b)] * alpha[w : w + 1, cols(b)]).astype(BF16)

    def gather(pairs, other, w):
        bs = reach(w)
        at = slice(bs[0] * COLS, (bs[-1] + 1) * COLS)
        return dot(pairs[cut(w), at], other[at, :])

    def back(src, dst, i, shift):
        return pltpu.make_async_remote_copy(
            src, dst, back_send.at[i], back_recv.at[i], device_id=to(shift), device_id_type=MESH
        )

    pv1 = back(pv.at[one], rv1, 0, -1)
    pv2 = back(pv.at[two], rv2, 1, -2)
    pk1 = back(pk.at[one], rk1, 2, -1)
    pk2 = back(pk.at[two], rk2, 3, -2)

    for w in range(7):
        for b in reach(w):
            prob(w, b)
    for w in range(3, 7):
        pv[cut(w), :] = gather(p_all, g_s, w).astype(BF16)

    @pl.when(prev1)
    def _():
        pv1.start()

    for w in range(3):
        pv[cut(w), :] = gather(p_all, g_s, w).astype(BF16)

    @pl.when(prev2)
    def _():
        pv2.start()

    for w in range(7, 11):
        for b in reach(w):
            prob(w, b)

    @pl.when(prev1)
    def _():
        v1.wait_recv()

    @pl.when(prev1 & next1 & even)
    def _():
        v2_on.start()

    turn(vwin, v_t, slice(ONE, ONE + TOK))

    @pl.when(prev2)
    def _():
        v2.wait_recv()

    turn(vwin, v_t, slice(0, 3 * BLK))

    def home(dst, b, x):
        for h in range(HEADS):
            dst[cut(b), cut(h)] = x[:, cut(h)].T

    for b in range(NB):
        keys = slice(b * BLK, (b + 8) * BLK)
        out = dot(v_t[:, keys], p_all[keys, cols(b)]).astype(BF16)
        delta[0:1, cols(b)] = jnp.sum(
            g_t[:, cols(b)].astype(F32) * out.astype(F32), axis=0, keepdims=True
        )
        home(att_out, b, out)

    def dscore(w, b):
        dp = dot(vwin[cut(w), :], g_t[:, cols(b)])
        d_all[cut(w), cols(b)] = (
            p_all[cut(w), cols(b)].astype(F32) * (dp - delta[0:1, cols(b)])
        ).astype(BF16)

    for w in range(7):
        for b in reach(w):
            dscore(w, b)
    for w in range(3, 7):
        pk[cut(w), :] = (gather(d_all, q_s, w) * SCALE).astype(BF16)

    @pl.when(prev1)
    def _():
        pk1.start()

    for w in range(3):
        pk[cut(w), :] = (gather(d_all, q_s, w) * SCALE).astype(BF16)

    @pl.when(prev2)
    def _():
        pk2.start()

    for w in range(7, 11):
        for b in reach(w):
            dscore(w, b)
    for b in range(NB):
        keys = slice(b * BLK, (b + 8) * BLK)
        home(qg_out, b, (dot(k_t[:, keys], d_all[keys, cols(b)]) * SCALE).astype(BF16))
    for w in range(7, 11):
        dk_own[cut(w - 7), :] = gather(d_all, q_s, w) * SCALE
        dv_own[cut(w - 7), :] = gather(p_all, g_s, w)

    @pl.when(next1)
    def _():
        pv1.wait_recv()
        dv_own[...] += rv1[...].astype(F32)

    @pl.when(next2)
    def _():
        pv2.wait_recv()
        dv_own[tail] += rv2[...].astype(F32)

    vg_out[...] = dv_own[...].astype(BF16)

    @pl.when(next1)
    def _():
        pk1.wait_recv()
        dk_own[...] += rk1[...].astype(F32)

    @pl.when(next2)
    def _():
        pk2.wait_recv()
        dk_own[tail] += rk2[...].astype(F32)

    kg_out[...] = dk_own[...].astype(BF16)

    @pl.when(next1)
    def _():
        k1.wait_send()
        v1.wait_send()

    @pl.when(next2 & even)
    def _():
        k2.wait_send()
        v2.wait_send()

    @pl.when(prev1 & next1 & even)
    def _():
        k2_on.wait_send()
        v2_on.wait_send()

    @pl.when(prev1)
    def _():
        pv1.wait_send()
        pk1.wait_send()

    @pl.when(prev2)
    def _():
        pv2.wait_send()
        pk2.wait_send()


def place(*refs):
    sems = refs[-1]
    half = (len(refs) - 1) // 2
    stores = [
        pltpu.make_async_copy(refs[i], refs[half + i], sems.at[i]) for i in range(half)
    ]
    for store in stores:
        store.start()
    for store in stores:
        store.wait()


def body(n, queries, key_vecs, value_vecs, out_grad, doc_ids):
    def buf(rows, columns, kind=BF16):
        return pltpu.VMEM((rows, columns), kind)

    wide = NB * COLS
    anywhere = pl.BlockSpec(memory_space=pl.ANY)
    in_vmem = pl.BlockSpec(memory_space=pltpu.VMEM)
    sizes = [(TOK, HEADS * HD), (TOK, HEADS * HD), (TOK, HD), (TOK, HD)]
    results = pl.pallas_call(
        functools.partial(kernel, n),
        name="attention",
        out_shape=[pltpu.VMEM(size, BF16) for size in sizes],
        in_specs=[pl.BlockSpec(memory_space=pltpu.SMEM)] + [anywhere] * 4,
        out_specs=[in_vmem] * 4,
        scratch_shapes=[
            buf(TOK, HEADS * HD), buf(TOK, HEADS * HD),
            buf(WIN * BLK, HD), buf(WIN * BLK, HD), buf(HD, WIN * BLK), buf(HD, WIN * BLK),
            buf(HD, wide), buf(HD, wide), buf(wide, HD), buf(wide, HD),
            buf(WIN * BLK, wide, F32), buf(WIN * BLK, wide), buf(WIN * BLK, wide),
            buf(16, wide, F32), buf(16, wide, F32), buf(16, wide, F32), buf(8, wide, F32),
            buf(TOK, HD, F32), buf(TOK, HD, F32),
            buf(7 * BLK, HD), buf(7 * BLK, HD),
            buf(TOK, HD), buf(3 * BLK, HD), buf(TOK, HD), buf(3 * BLK, HD),
            pltpu.SemaphoreType.DMA((4,)), pltpu.SemaphoreType.DMA((4,)),
            pltpu.SemaphoreType.DMA((4,)), pltpu.SemaphoreType.DMA((4,)),
            pltpu.SemaphoreType.DMA((4,)),
        ],
        compiler_params=pltpu.CompilerParams(
            collective_id=0, has_side_effects=True, vmem_limit_bytes=56 * 1024 * 1024
        ),
        cost_estimate=pl.CostEstimate(
            flops=2 * 6 * 32 * HEADS * BLK**3, bytes_accessed=5 * TOK * TOK, transcendentals=2**21
        ),
    )(doc_ids, queries, key_vecs, value_vecs, out_grad)
    results = [pltpu.with_memory_space_constraint(r, pltpu.VMEM) for r in results]
    return pl.pallas_call(
        place,
        name="place",
        out_shape=[jax.ShapeDtypeStruct(size, BF16) for size in sizes],
        in_specs=[in_vmem] * 4,
        out_specs=[anywhere] * 4,
        scratch_shapes=[pltpu.SemaphoreType.DMA((4,))],
    )(*results)


def solution(mesh):
    placed = P("ctx", "tp")
    return jax.shard_map(
        functools.partial(body, mesh.shape["ctx"]),
        mesh=mesh,
        in_specs=(placed,) * 4 + (P(),),
        out_specs=(placed,) * 4,
        check_vma=False,
    )
```

time: 78.1 us -> 37.7 us (0.48)
  Pallas kernels: 0 us -> 36.9 us
  waiting for transfers between devices: 29.4 us -> 0 us
  matrix products: 20.1 us -> 0 us
  starting transfers between devices: 17.1 us -> 0 us
  local copies, waits for them, and re-layouts: 5.1 us -> 0 us
  other arithmetic: 5.09 us -> 0 us
    pallas_call x0 -> x2, Pallas kernels: none -> 36.9 us  [the longest x1 35.8 us: body(): pl.pallas_call(functools.partial(kernel, n), name='attention', out_shape=...]
    ppermute x4 -> x0, waiting for transfers between devices: 29.4 us -> none  [from_behind(): return lax.ppermute(block, axis, route)]
    dot_general x18 -> x0, matrix products: 20.1 us -> none  [the longest x3 4.8 us: back_fn(): jnp.einsum('hgqk,qhgd->khd', probs16[offset], grad_split, preferred_eleme...]
    ppermute x4 -> x0, starting transfers between devices: 17.1 us -> none  [from_behind(): return lax.ppermute(block, axis, route)]
    reduce_sum x1 -> x0, other arithmetic: 2.75 us -> none  [body(): jnp.sum(jnp.where(masks[o], jnp.exp(scores[o] - highest), 0.0), axis=-1,...]
    unnamed x14 -> x0, local copies, waits for them, and re-layouts: 2.06 us -> none
    convert_element_type x2 -> x0, local copies, waits for them, and re-layouts: 1.97 us -> none  [the longest x1 1.25 us: body(): grad_split.astype(jnp.float32) * output16.astype(jnp.float32)]
    another operation x3 -> x0, other arithmetic: 1.14 us -> none  [the longest x1 1.05 us: body(): own_pair = jnp.stack([key_vecs, value_vecs])]
  transfers between devices with their start and end apart: 4 -> 0, of which waited for: 4 -> 0; matrix products, arithmetic and copies ran while one was open for 22% -> 0% of each run, Pallas kernels for 0% -> 0%
where the time goes in v1:
time: 37.7 us; the launch traced here: 37.5 us
  Pallas kernels  36.9 us (98%)
  between operations  0.64 us (2%)
    pallas_call x1, Pallas kernels, body(): pl.pallas_call(functools.partial(kernel, n), name='attention', out_shape=...  35.8 us
    pallas_call x1, Pallas kernels, body(): pl.pallas_call(place, name='place', out_shape=[jax.ShapeDtypeStruct(size,...  1.08 us

profile of v1, /device:TPU:50, one launch (start us, length us, event | category | flops | bytes accessed | tf_op | source)
XLA Modules:
  0.0 37.5 jit_solution(5353760489286155411)
XLA Ops:
  0.6 35.8 %attention.1 = (bf16[512,512]{1,0:T(8,128)(2,1)S(1)}, bf16[512,512]{1,0:T(8,128)(2,1)S(1)}, bf16[512,128]{1,0:T(8,128)(2,1)S(1)}, bf16[512,128]{1,0:T(8,128)(2,1)S(1)}) custom-call(s32[384]{0:T(512)} %docs.1, bf16[512,512]{1,0:T(8,128)(2,1)} %q_hbm.1, bf16[512,128]{1,0:T(8,128)(2,1)} %k_hbm.1, bf16[512,128]{1,0:T(8,128)(2,1)} %v_hbm.1, bf16[512,512]{1,0:T(8,128)(2,1)} %g_hbm.1), custom_call_target="tpu_custom_call" | custom-call | flops 3221225472 | bytes 1310720 | tf_op jit(solution)/shard_map/attention/pallas_call | solution.py:371
  36.4 1.1 %place.1 = (bf16[512,512]{1,0:T(8,128)(2,1)}, bf16[512,512]{1,0:T(8,128)(2,1)}, bf16[512,128]{1,0:T(8,128)(2,1)}, bf16[512,128]{1,0:T(8,128)(2,1)}) custom-call(bf16[512,512]{1,0:T(8,128)(2,1)S(1)} %get-tuple-element.8.refs_0_, bf16[512,512]{1,0:T(8,128)(2,1)S(1)} %get-tuple-element.9.refs_1_, bf16[512,128]{1,0:T(8,128)(2,1)S(1)} %get-tuple-element.10.refs_2_, ...), custom_call_target="tpu_custom_call" | custom-call | tf_op jit(solution)/shard_map/place/pallas_call | solution.py:398

commit v2 on v1

--- a/solution.py
+++ b/solution.py
@@ -15,6 +15,7 @@
 TOK = NB * BLK
 WIN = 11
 COLS = HEADS * BLK
+COLUMN = 24
 OWN = 7 * BLK
 ONE = 3 * BLK
 SCALE = HD**-0.5
@@ -34,14 +35,21 @@
     att_out, qg_out, kg_out, vg_out,
     q_in, g_in,
     kwin, vwin, k_t, v_t, q_t, g_t, q_s, g_s,
-    e_all, p_all, d_all, top, total, alpha, delta,
+    e_all, p_all, d_all, dp_own, out_own, top, total, alpha, delta,
     dk_own, dv_own, pk, pv, rk1, rk2, rv1, rv2,
     load_sem, send_sem, recv_sem, back_send, back_recv,
+    v_hop, pv_hop, pk_hop, v_hop_send, v_hop_recv, hop_send, hop_recv, ready,
 ):
     s = lax.axis_index("ctx")
     even = lax.rem(s, 2) == 0
     odd = lax.rem(s, 2) == 1
     prev1, prev2, next1, next2 = s >= 1, s >= 2, s + 1 < n, s + 2 < n
+    place_in = lax.rem(s, COLUMN)
+    high = lax.rem(lax.axis_index("tp"), 2) == 1
+    first = high & (place_in < 2) & (s >= COLUMN)
+    v_passes = high & (place_in >= 2) & (place_in < 4) & (s >= COLUMN)
+    passes = high & (place_in >= COLUMN - 4) & (place_in < COLUMN - 2) & (s + 4 < n)
+    v_far = high & (place_in >= COLUMN - 2) & (s + 4 < n)
 
     def to(shift):
         return {"ctx": lax.rem(s + shift + n, n)}
@@ -55,6 +63,10 @@
     @pl.when(prev2 & even)
     def _():
         pl.semaphore_signal(barrier, inc=1, device_id=to(-2), device_id_type=MESH)
+
+    @pl.when(first | v_passes)
+    def _():
+        pl.semaphore_signal(barrier, inc=1, device_id=to(-4), device_id_type=MESH)
 
     own = pl.ds(OWN, TOK)
     load_q = pltpu.make_async_copy(q_hbm, q_in, load_sem.at[0])
@@ -62,11 +74,17 @@
     load_v = pltpu.make_async_copy(v_hbm, vwin.at[own], load_sem.at[2])
     load_g = pltpu.make_async_copy(g_hbm, g_in, load_sem.at[3])
 
-    targets = next1.astype(jnp.int32) + (next2 & even).astype(jnp.int32)
+    targets = sum(
+        x.astype(jnp.int32) for x in (next1, next2 & even, passes, v_far)
+    )
 
     @pl.when(targets > 0)
     def _():
         pl.semaphore_wait(barrier, targets)
+
+    @pl.when(passes)
+    def _():
+        pl.semaphore_signal(ready, inc=1, device_id=to(4), device_id_type=MESH)
 
     def send(src, dst, i, shift):
         return pltpu.make_async_remote_copy(
@@ -90,11 +108,39 @@
     def _():
         k2.start()
 
-    @pl.when(next1)
+    def v_up(src, i, j):
+        return pltpu.make_async_remote_copy(
+            v_hbm.at[src], v_hop.at[src], send_sem.at[i], v_hop_recv.at[j],
+            device_id=to(4), device_id_type=MESH,
+        )
+
+    def v_over(src, dst, i, j, shift):
+        return pltpu.make_async_remote_copy(
+            v_hop.at[src], vwin.at[dst], v_hop_send.at[j], recv_sem.at[i],
+            device_id=to(shift), device_id_type=MESH,
+        )
+
+    blocks = [pl.ds(j * BLK, BLK) for j in range(7)]
+    v1_up = [v_up(blocks[j], 2, j) for j in (1, 2, 3, 0)]
+    v1_over = [v_over(blocks[j], blocks[3 + j], 2, j, -3) for j in (1, 2, 3, 0)]
+    v2_up = [v_up(blocks[j], 3, j) for j in (1, 2, 3)]
+    v2_over = [v_over(blocks[j], blocks[j - 1], 3, j, -2) for j in (1, 2, 3)]
+
+    @pl.when(v_far & odd)
+    def _():
+        for copy in v1_up:
+            copy.start()
+
+    @pl.when(v_far & even)
+    def _():
+        for copy in v2_up:
+            copy.start()
+
+    @pl.when(next1 & jnp.logical_not(v_far & odd))
     def _():
         v1.start()
 
-    @pl.when(next2 & even)
+    @pl.when(next2 & even & jnp.logical_not(v_far))
     def _():
         v2.start()
 
@@ -156,6 +202,9 @@
     split(g_in, g_s, g_t)
     load_v.wait()
     turn(vwin, v_t, slice(OWN, OWN + TOK))
+    for w in range(7, 11):
+        for b in reach(w):
+            dp_own[cut(w - 7), cols(b)] = dot(vwin[cut(w), :], g_t[:, cols(b)])
 
     @pl.when(prev1)
     def _():
@@ -216,35 +265,68 @@
     pk1 = back(pk.at[one], rk1, 2, -1)
     pk2 = back(pk.at[two], rk2, 3, -2)
 
+    def hop(src, dst, i):
+        return pltpu.make_async_remote_copy(
+            src, dst, back_send.at[i], hop_recv.at[i],
+            device_id=to(-4), device_id_type=MESH,
+        )
+
+    def over(src, dst, i, shift):
+        return pltpu.make_async_remote_copy(
+            src, dst, hop_send.at[i], back_recv.at[i], device_id=to(shift), device_id_type=MESH
+        )
+
+    pv1_hop = hop(pv.at[one], pv_hop.at[one], 0)
+    pv2_hop = hop(pv.at[two], pv_hop.at[two], 1)
+    pk1_hop = hop(pk.at[one], pk_hop.at[one], 2)
+    pk2_hop = hop(pk.at[two], pk_hop.at[two], 3)
+    pv1_over = over(pv_hop.at[one], rv1, 0, 3)
+    pv2_over = over(pv_hop.at[two], rv2, 1, 2)
+    pk1_over = over(pk_hop.at[one], rk1, 2, 3)
+    pk2_over = over(pk_hop.at[two], rk2, 3, 2)
+
     for w in range(7):
         for b in reach(w):
             prob(w, b)
-    for w in range(3, 7):
-        pv[cut(w), :] = gather(p_all, g_s, w).astype(BF16)
-
-    @pl.when(prev1)
+    pv[3 * BLK :, :] = dot(p_all[3 * BLK : 7 * BLK, :], g_s[...]).astype(BF16)
+
+    @pl.when(first)
+    def _():
+        pl.semaphore_wait(ready, 1)
+
+    @pl.when(first & even)
+    def _():
+        pv1_hop.start()
+
+    @pl.when(prev1 & jnp.logical_not(first & even))
     def _():
         pv1.start()
 
     for w in range(3):
         pv[cut(w), :] = gather(p_all, g_s, w).astype(BF16)
 
-    @pl.when(prev2)
+    @pl.when(first)
+    def _():
+        pv2_hop.start()
+
+    @pl.when(prev2 & jnp.logical_not(first))
     def _():
         pv2.start()
 
+    @pl.when(prev1)
+    def _():
+        v1.wait_recv()
+
+    @pl.when(prev1 & next1 & even)
+    def _():
+        v2_on.start()
+
     for w in range(7, 11):
         for b in reach(w):
             prob(w, b)
-
-    @pl.when(prev1)
-    def _():
-        v1.wait_recv()
-
-    @pl.when(prev1 & next1 & even)
-    def _():
-        v2_on.start()
-
+    for b in range(NB):
+        keys = slice(OWN, OWN + (b + 1) * BLK)
+        out_own[:, cols(b)] = dot(v_t[:, keys], p_all[keys, cols(b)])
     turn(vwin, v_t, slice(ONE, ONE + TOK))
 
     @pl.when(prev2)
@@ -258,15 +340,18 @@
             dst[cut(b), cut(h)] = x[:, cut(h)].T
 
     for b in range(NB):
-        keys = slice(b * BLK, (b + 8) * BLK)
-        out = dot(v_t[:, keys], p_all[keys, cols(b)]).astype(BF16)
+        keys = slice(b * BLK, OWN)
+        out = (dot(v_t[:, keys], p_all[keys, cols(b)]) + out_own[:, cols(b)]).astype(BF16)
         delta[0:1, cols(b)] = jnp.sum(
             g_t[:, cols(b)].astype(F32) * out.astype(F32), axis=0, keepdims=True
         )
         home(att_out, b, out)
 
     def dscore(w, b):
-        dp = dot(vwin[cut(w), :], g_t[:, cols(b)])
+        if w < 7:
+            dp = dot(vwin[cut(w), :], g_t[:, cols(b)])
+        else:
+            dp = dp_own[cut(w - 7), cols(b)]
         d_all[cut(w), cols(b)] = (
             p_all[cut(w), cols(b)].astype(F32) * (dp - delta[0:1, cols(b)])
         ).astype(BF16)
@@ -274,17 +359,24 @@
     for w in range(7):
         for b in reach(w):
             dscore(w, b)
-    for w in range(3, 7):
-        pk[cut(w), :] = (gather(d_all, q_s, w) * SCALE).astype(BF16)
-
-    @pl.when(prev1)
+    pk[3 * BLK :, :] = (dot(d_all[3 * BLK : 7 * BLK, :], q_s[...]) * SCALE).astype(BF16)
+
+    @pl.when(first & even)
+    def _():
+        pk1_hop.start()
+
+    @pl.when(prev1 & jnp.logical_not(first & even))
     def _():
         pk1.start()
 
     for w in range(3):
         pk[cut(w), :] = (gather(d_all, q_s, w) * SCALE).astype(BF16)
 
-    @pl.when(prev2)
+    @pl.when(first)
+    def _():
+        pk2_hop.start()
+
+    @pl.when(prev2 & jnp.logical_not(first))
     def _():
         pk2.start()
 
@@ -298,6 +390,38 @@
         dk_own[cut(w - 7), :] = gather(d_all, q_s, w) * SCALE
         dv_own[cut(w - 7), :] = gather(p_all, g_s, w)
 
+    @pl.when(v_passes & odd)
+    def _():
+        for arrives, leaves in zip(v1_up, v1_over):
+            arrives.wait_recv()
+            leaves.start()
+
+    @pl.when(v_passes & even)
+    def _():
+        for arrives, leaves in zip(v2_up, v2_over):
+            arrives.wait_recv()
+            leaves.start()
+
+    @pl.when(passes & even)
+    def _():
+        pv1_hop.wait_recv()
+        pv1_over.start()
+
+    @pl.when(passes)
+    def _():
+        pv2_hop.wait_recv()
+        pv2_over.start()
+
+    @pl.when(passes & even)
+    def _():
+        pk1_hop.wait_recv()
+        pk1_over.start()
+
+    @pl.when(passes)
+    def _():
+        pk2_hop.wait_recv()
+        pk2_over.start()
+
     @pl.when(next1)
     def _():
         pv1.wait_recv()
@@ -346,6 +470,26 @@
     def _():
         pv2.wait_send()
         pk2.wait_send()
+
+    @pl.when(v_passes & odd)
+    def _():
+        for copy in v1_over:
+            copy.wait_send()
+
+    @pl.when(v_passes & even)
+    def _():
+        for copy in v2_over:
+            copy.wait_send()
+
+    @pl.when(passes & even)
+    def _():
+        pv1_over.wait_send()
+        pk1_over.wait_send()
+
+    @pl.when(passes)
+    def _():
+        pv2_over.wait_send()
+        pk2_over.wait_send()
 
 
 def place(*refs):
@@ -379,6 +523,7 @@
             buf(WIN * BLK, HD), buf(WIN * BLK, HD), buf(HD, WIN * BLK), buf(HD, WIN * BLK),
             buf(HD, wide), buf(HD, wide), buf(wide, HD), buf(wide, HD),
             buf(WIN * BLK, wide, F32), buf(WIN * BLK, wide), buf(WIN * BLK, wide),
+            buf(TOK, wide, F32), buf(HD, wide, F32),
             buf(16, wide, F32), buf(16, wide, F32), buf(16, wide, F32), buf(8, wide, F32),
             buf(TOK, HD, F32), buf(TOK, HD, F32),
             buf(7 * BLK, HD), buf(7 * BLK, HD),
@@ -386,6 +531,10 @@
             pltpu.SemaphoreType.DMA((4,)), pltpu.SemaphoreType.DMA((4,)),
             pltpu.SemaphoreType.DMA((4,)), pltpu.SemaphoreType.DMA((4,)),
             pltpu.SemaphoreType.DMA((4,)),
+            buf(TOK, HD), buf(7 * BLK, HD), buf(7 * BLK, HD),
+            pltpu.SemaphoreType.DMA((4,)), pltpu.SemaphoreType.DMA((4,)),
+            pltpu.SemaphoreType.DMA((4,)), pltpu.SemaphoreType.DMA((4,)),
+            pltpu.SemaphoreType.REGULAR,
         ],
         compiler_params=pltpu.CompilerParams(
             collective_id=0, has_side_effects=True, vmem_limit_bytes=56 * 1024 * 1024

time: 37.7 us -> 34.4 us (0.912)
  the two profiles are of different devices: /device:TPU:50 before, /device:TPU:48 now
where the time goes in v2:
time: 34.4 us; the launch traced here: 34.2 us
  Pallas kernels  33.6 us (98%)
  between operations  0.64 us (2%)
    pallas_call x1, Pallas kernels, body(): pl.pallas_call(functools.partial(kernel, n), name='attention', out_shape=...  32.5 us
    pallas_call x1, Pallas kernels, body(): pl.pallas_call(place, name='place', out_shape=[jax.ShapeDtypeStruct(size,...  1.08 us

profile of v2, /device:TPU:48, one launch (start us, length us, event | category | flops | bytes accessed | tf_op | source)
XLA Modules:
  0.0 34.2 jit_solution(5129242877750511796)
XLA Ops:
  0.6 32.5 %attention.1 = (bf16[512,512]{1,0:T(8,128)(2,1)S(1)}, bf16[512,512]{1,0:T(8,128)(2,1)S(1)}, bf16[512,128]{1,0:T(8,128)(2,1)S(1)}, bf16[512,128]{1,0:T(8,128)(2,1)S(1)}) custom-call(s32[384]{0:T(512)} %docs.1, bf16[512,512]{1,0:T(8,128)(2,1)} %q_hbm.1, bf16[512,128]{1,0:T(8,128)(2,1)} %k_hbm.1, bf16[512,128]{1,0:T(8,128)(2,1)} %v_hbm.1, bf16[512,512]{1,0:T(8,128)(2,1)} %g_hbm.1), custom_call_target="tpu_custom_call" | custom-call | flops 3221225472 | bytes 1310720 | tf_op jit(solution)/shard_map/attention/pallas_call | solution.py:515
  33.1 1.1 %place.1 = (bf16[512,512]{1,0:T(8,128)(2,1)}, bf16[512,512]{1,0:T(8,128)(2,1)}, bf16[512,128]{1,0:T(8,128)(2,1)}, bf16[512,128]{1,0:T(8,128)(2,1)}) custom-call(bf16[512,512]{1,0:T(8,128)(2,1)S(1)} %get-tuple-element.8.refs_0_, bf16[512,512]{1,0:T(8,128)(2,1)S(1)} %get-tuple-element.9.refs_1_, bf16[512,128]{1,0:T(8,128)(2,1)S(1)} %get-tuple-element.10.refs_2_, ...), custom_call_target="tpu_custom_call" | custom-call | tf_op jit(solution)/shard_map/place/pallas_call | solution.py:547

commit v3 on v2

--- a/solution.py
+++ b/solution.py
@@ -86,27 +86,63 @@
     def _():
         pl.semaphore_signal(ready, inc=1, device_id=to(4), device_id_type=MESH)
 
-    def send(src, dst, i, shift):
+    def send(src, dst, i, arrival, shift):
         return pltpu.make_async_remote_copy(
-            src, dst, send_sem.at[i], recv_sem.at[i], device_id=to(shift), device_id_type=MESH
-        )
-
+            src, dst, send_sem.at[i], recv_sem.at[arrival],
+            device_id=to(shift), device_id_type=MESH,
+        )
+
+    blocks = [pl.ds(j * BLK, BLK) for j in range(7)]
     tail = pl.ds(BLK, 3 * BLK)
-    one, two, one_tail = pl.ds(ONE, TOK), pl.ds(0, 3 * BLK), pl.ds(ONE + BLK, 3 * BLK)
-    k1 = send(k_hbm, kwin.at[one], 0, 1)
-    v1 = send(v_hbm, vwin.at[one], 2, 1)
-    k2 = send(k_hbm.at[tail], kwin.at[two], 1, 2)
-    v2 = send(v_hbm.at[tail], vwin.at[two], 3, 2)
-    k2_on = send(kwin.at[one_tail], kwin.at[two], 1, 1)
-    v2_on = send(vwin.at[one_tail], vwin.at[two], 3, 1)
+    one, two = pl.ds(ONE, TOK), pl.ds(0, 3 * BLK)
+    order = (1, 2, 3, 0)
+
+    def stream(hbm, win, i):
+        to_one = {j: send(hbm.at[blocks[j]], win.at[blocks[3 + j]], i, 7 * i + j, 1) for j in order}
+        to_two = {
+            j: send(hbm.at[blocks[j]], win.at[blocks[j - 1]], 2 + i, 7 * i + 3 + j, 2)
+            for j in order[:3]
+        }
+        onward = {
+            j: send(win.at[blocks[3 + j]], win.at[blocks[j - 1]], 4 + i, 7 * i + 3 + j, 1)
+            for j in order[:3]
+        }
+        return to_one, to_two, onward
+
+    k1, k2, k2_on = stream(k_hbm, kwin, 0)
+    v1, v2, v2_on = stream(v_hbm, vwin, 1)
+
+    def start(copies):
+        for copy in copies.values():
+            copy.start()
+
+    def left(copies):
+        for copy in copies.values():
+            copy.wait_send()
+
+    def arrived_one(copies, onward, j):
+        @pl.when(prev1)
+        def _():
+            copies[j].wait_recv()
+
+        if j > 0:
+
+            @pl.when(prev1 & next1 & even)
+            def _():
+                onward[j].start()
+
+    def arrived_two(copies, j):
+        @pl.when(prev2)
+        def _():
+            copies[j].wait_recv()
 
     @pl.when(next1)
     def _():
-        k1.start()
+        start(k1)
 
     @pl.when(next2 & even)
     def _():
-        k2.start()
+        start(k2)
 
     def v_up(src, i, j):
         return pltpu.make_async_remote_copy(
@@ -120,11 +156,10 @@
             device_id=to(shift), device_id_type=MESH,
         )
 
-    blocks = [pl.ds(j * BLK, BLK) for j in range(7)]
-    v1_up = [v_up(blocks[j], 2, j) for j in (1, 2, 3, 0)]
-    v1_over = [v_over(blocks[j], blocks[3 + j], 2, j, -3) for j in (1, 2, 3, 0)]
-    v2_up = [v_up(blocks[j], 3, j) for j in (1, 2, 3)]
-    v2_over = [v_over(blocks[j], blocks[j - 1], 3, j, -2) for j in (1, 2, 3)]
+    v1_up = [v_up(blocks[j], 1, j) for j in order]
+    v1_over = [v_over(blocks[j], blocks[3 + j], 7 + j, j, -3) for j in order]
+    v2_up = [v_up(blocks[j], 3, j) for j in order[:3]]
+    v2_over = [v_over(blocks[j], blocks[j - 1], 10 + j, j, -2) for j in order[:3]]
 
     @pl.when(v_far & odd)
     def _():
@@ -138,11 +173,11 @@
 
     @pl.when(next1 & jnp.logical_not(v_far & odd))
     def _():
-        v1.start()
+        start(v1)
 
     @pl.when(next2 & even & jnp.logical_not(v_far))
     def _():
-        v2.start()
+        start(v2)
 
     for load in (load_q, load_k, load_g, load_v):
         load.start()
@@ -206,27 +241,24 @@
         for b in reach(w):
             dp_own[cut(w - 7), cols(b)] = dot(vwin[cut(w), :], g_t[:, cols(b)])
 
-    @pl.when(prev1)
-    def _():
-        k1.wait_recv()
-
-    @pl.when(prev1 & next1 & even)
-    def _():
-        k2_on.start()
-
-    for b in range(NB):
-        for w in range(3, 7):
-            score(w, b)
-    turn(kwin, k_t, slice(ONE, ONE + TOK))
-
-    @pl.when(prev2)
-    def _():
-        k2.wait_recv()
-
-    for w in range(3):
-        for b in reach(w):
-            score(w, b)
-    turn(kwin, k_t, slice(0, 3 * BLK))
+    def score_one(j):
+        arrived_one(k1, k2_on, j)
+        for b in range(NB):
+            score(3 + j, b)
+
+    def score_two(j):
+        arrived_two(k2, j)
+        for b in reach(j - 1):
+            score(j - 1, b)
+
+    score_one(1)
+    score_one(2)
+    score_two(1)
+    score_one(3)
+    score_two(2)
+    score_two(3)
+    score_one(0)
+    turn(kwin, k_t, slice(0, OWN))
 
     for b in range(NB):
         mine = docs[s * NB + b]
@@ -285,42 +317,37 @@
     pk1_over = over(pk_hop.at[one], rk1, 2, 3)
     pk2_over = over(pk_hop.at[two], rk2, 3, 2)
 
-    for w in range(7):
+    for w in range(3):
         for b in reach(w):
             prob(w, b)
-    pv[3 * BLK :, :] = dot(p_all[3 * BLK : 7 * BLK, :], g_s[...]).astype(BF16)
-
-    @pl.when(first)
-    def _():
-        pl.semaphore_wait(ready, 1)
-
-    @pl.when(first & even)
-    def _():
-        pv1_hop.start()
-
-    @pl.when(prev1 & jnp.logical_not(first & even))
-    def _():
-        pv1.start()
-
     for w in range(3):
         pv[cut(w), :] = gather(p_all, g_s, w).astype(BF16)
 
     @pl.when(first)
     def _():
+        pl.semaphore_wait(ready, 1)
         pv2_hop.start()
 
     @pl.when(prev2 & jnp.logical_not(first))
     def _():
         pv2.start()
 
-    @pl.when(prev1)
-    def _():
-        v1.wait_recv()
-
-    @pl.when(prev1 & next1 & even)
-    def _():
-        v2_on.start()
-
+    for w in range(3, 7):
+        for b in range(NB):
+            prob(w, b)
+    for w in range(3, 7):
+        pv[cut(w), :] = gather(p_all, g_s, w).astype(BF16)
+
+    @pl.when(first & even)
+    def _():
+        pv1_hop.start()
+
+    @pl.when(prev1 & jnp.logical_not(first & even))
+    def _():
+        pv1.start()
+
+    for j in order:
+        arrived_one(v1, v2_on, j)
     for w in range(7, 11):
         for b in reach(w):
             prob(w, b)
@@ -329,9 +356,8 @@
         out_own[:, cols(b)] = dot(v_t[:, keys], p_all[keys, cols(b)])
     turn(vwin, v_t, slice(ONE, ONE + TOK))
 
-    @pl.when(prev2)
-    def _():
-        v2.wait_recv()
+    for j in order[:3]:
+        arrived_two(v2, j)
 
     turn(vwin, v_t, slice(0, 3 * BLK))
 
@@ -359,7 +385,8 @@
     for w in range(7):
         for b in reach(w):
             dscore(w, b)
-    pk[3 * BLK :, :] = (dot(d_all[3 * BLK : 7 * BLK, :], q_s[...]) * SCALE).astype(BF16)
+    for w in range(3, 7):
+        pk[cut(w), :] = (gather(d_all, q_s, w) * SCALE).astype(BF16)
 
     @pl.when(first & even)
     def _():
@@ -448,18 +475,18 @@
 
     @pl.when(next1)
     def _():
-        k1.wait_send()
-        v1.wait_send()
+        left(k1)
+        left(v1)
 
     @pl.when(next2 & even)
     def _():
-        k2.wait_send()
-        v2.wait_send()
+        left(k2)
+        left(v2)
 
     @pl.when(prev1 & next1 & even)
     def _():
-        k2_on.wait_send()
-        v2_on.wait_send()
+        left(k2_on)
+        left(v2_on)
 
     @pl.when(prev1)
     def _():
@@ -528,9 +555,8 @@
             buf(TOK, HD, F32), buf(TOK, HD, F32),
             buf(7 * BLK, HD), buf(7 * BLK, HD),
             buf(TOK, HD), buf(3 * BLK, HD), buf(TOK, HD), buf(3 * BLK, HD),
+            pltpu.SemaphoreType.DMA((4,)), pltpu.SemaphoreType.DMA((6,)), pltpu.SemaphoreType.DMA((14,)),
             pltpu.SemaphoreType.DMA((4,)), pltpu.SemaphoreType.DMA((4,)),
-            pltpu.SemaphoreType.DMA((4,)), pltpu.SemaphoreType.DMA((4,)),
-            pltpu.SemaphoreType.DMA((4,)),
             buf(TOK, HD), buf(7 * BLK, HD), buf(7 * BLK, HD),
             pltpu.SemaphoreType.DMA((4,)), pltpu.SemaphoreType.DMA((4,)),
             pltpu.SemaphoreType.DMA((4,)), pltpu.SemaphoreType.DMA((4,)),

time: 34.4 us -> 33.4 us (0.971)
  the two profiles are of different devices: /device:TPU:48 before, /device:TPU:58 now
where the time goes in v3:
time: 33.4 us; the launch traced here: 33.2 us
  Pallas kernels  32.5 us (97%)
  between operations  0.64 us (2%)
    pallas_call x1, Pallas kernels, body(): pl.pallas_call(functools.partial(kernel, n), name='attention', out_shape=...  31.5 us
    pallas_call x1, Pallas kernels, body(): pl.pallas_call(place, name='place', out_shape=[jax.ShapeDtypeStruct(size,...  1.08 us

profile of v3, /device:TPU:58, one launch (start us, length us, event | category | flops | bytes accessed | tf_op | source)
XLA Modules:
  0.0 33.2 jit_solution(4127144626261132089)
XLA Ops:
  0.6 31.5 %attention.1 = (bf16[512,512]{1,0:T(8,128)(2,1)S(1)}, bf16[512,512]{1,0:T(8,128)(2,1)S(1)}, bf16[512,128]{1,0:T(8,128)(2,1)S(1)}, bf16[512,128]{1,0:T(8,128)(2,1)S(1)}) custom-call(s32[384]{0:T(512)} %docs.1, bf16[512,512]{1,0:T(8,128)(2,1)} %q_hbm.1, bf16[512,128]{1,0:T(8,128)(2,1)} %k_hbm.1, bf16[512,128]{1,0:T(8,128)(2,1)} %v_hbm.1, bf16[512,512]{1,0:T(8,128)(2,1)} %g_hbm.1), custom_call_target="tpu_custom_call" | custom-call | flops 3221225472 | bytes 1310720 | tf_op jit(solution)/shard_map/attention/pallas_call | solution.py:542
  32.1 1.1 %place.1 = (bf16[512,512]{1,0:T(8,128)(2,1)}, bf16[512,512]{1,0:T(8,128)(2,1)}, bf16[512,128]{1,0:T(8,128)(2,1)}, bf16[512,128]{1,0:T(8,128)(2,1)}) custom-call(bf16[512,512]{1,0:T(8,128)(2,1)S(1)} %get-tuple-element.8.refs_0_, bf16[512,512]{1,0:T(8,128)(2,1)S(1)} %get-tuple-element.9.refs_1_, bf16[512,128]{1,0:T(8,128)(2,1)S(1)} %get-tuple-element.10.refs_2_, ...), custom_call_target="tpu_custom_call" | custom-call | tf_op jit(solution)/shard_map/place/pallas_call | solution.py:573

commit v4 on v3

--- a/solution.py
+++ b/solution.py
@@ -297,6 +297,18 @@
     pk1 = back(pk.at[one], rk1, 2, -1)
     pk2 = back(pk.at[two], rk2, 3, -2)
 
+    def leave(part, one_dst, hop_dst, i, w):
+        direct = back(part.at[blocks[w]], one_dst.at[blocks[w - 3]], i, -1)
+        by_hop = hop(part.at[blocks[w]], hop_dst.at[blocks[w]], i)
+
+        @pl.when(first & even)
+        def _():
+            by_hop.start()
+
+        @pl.when(prev1 & jnp.logical_not(first & even))
+        def _():
+            direct.start()
+
     def hop(src, dst, i):
         return pltpu.make_async_remote_copy(
             src, dst, back_send.at[i], hop_recv.at[i],
@@ -335,19 +347,13 @@
     for w in range(3, 7):
         for b in range(NB):
             prob(w, b)
-    for w in range(3, 7):
         pv[cut(w), :] = gather(p_all, g_s, w).astype(BF16)
-
-    @pl.when(first & even)
-    def _():
-        pv1_hop.start()
-
-    @pl.when(prev1 & jnp.logical_not(first & even))
-    def _():
-        pv1.start()
-
-    for j in order:
-        arrived_one(v1, v2_on, j)
+        leave(pv, rv1, pv_hop, 0, w)
+        if w == 4:
+            arrived_one(v1, v2_on, 1)
+            arrived_one(v1, v2_on, 2)
+    arrived_one(v1, v2_on, 3)
+    arrived_one(v1, v2_on, 0)
     for w in range(7, 11):
         for b in reach(w):
             prob(w, b)
@@ -382,19 +388,9 @@
             p_all[cut(w), cols(b)].astype(F32) * (dp - delta[0:1, cols(b)])
         ).astype(BF16)
 
-    for w in range(7):
+    for w in range(3):
         for b in reach(w):
             dscore(w, b)
-    for w in range(3, 7):
-        pk[cut(w), :] = (gather(d_all, q_s, w) * SCALE).astype(BF16)
-
-    @pl.when(first & even)
-    def _():
-        pk1_hop.start()
-
-    @pl.when(prev1 & jnp.logical_not(first & even))
-    def _():
-        pk1.start()
 
     for w in range(3):
         pk[cut(w), :] = (gather(d_all, q_s, w) * SCALE).astype(BF16)
@@ -406,6 +402,12 @@
     @pl.when(prev2 & jnp.logical_not(first))
     def _():
         pk2.start()
+
+    for w in range(3, 7):
+        for b in range(NB):
+            dscore(w, b)
+        pk[cut(w), :] = (gather(d_all, q_s, w) * SCALE).astype(BF16)
+        leave(pk, rk1, pk_hop, 2, w)
 
     for w in range(7, 11):
         for b in reach(w):

time: 33.4 us -> 32.7 us (0.979)
  the two profiles are of different devices: /device:TPU:58 before, /device:TPU:53 now
where the time goes in v4:
time: 32.7 us; the launch traced here: 32.5 us
  Pallas kernels  31.9 us (98%)
  between operations  0.64 us (2%)
    pallas_call x1, Pallas kernels, body(): pl.pallas_call(functools.partial(kernel, n), name='attention', out_shape=...  30.8 us
    pallas_call x1, Pallas kernels, body(): pl.pallas_call(place, name='place', out_shape=[jax.ShapeDtypeStruct(size,...  1.08 us

profile of v4, /device:TPU:53, one launch (start us, length us, event | category | flops | bytes accessed | tf_op | source)
XLA Modules:
  0.0 32.5 jit_solution(13036718682943816424)
XLA Ops:
  0.6 30.8 %attention.1 = (bf16[512,512]{1,0:T(8,128)(2,1)S(1)}, bf16[512,512]{1,0:T(8,128)(2,1)S(1)}, bf16[512,128]{1,0:T(8,128)(2,1)S(1)}, bf16[512,128]{1,0:T(8,128)(2,1)S(1)}) custom-call(s32[384]{0:T(512)} %docs.1, bf16[512,512]{1,0:T(8,128)(2,1)} %q_hbm.1, bf16[512,128]{1,0:T(8,128)(2,1)} %k_hbm.1, bf16[512,128]{1,0:T(8,128)(2,1)} %v_hbm.1, bf16[512,512]{1,0:T(8,128)(2,1)} %g_hbm.1), custom_call_target="tpu_custom_call" | custom-call | flops 3221225472 | bytes 1310720 | tf_op jit(solution)/shard_map/attention/pallas_call | solution.py:544
  31.4 1.1 %place.1 = (bf16[512,512]{1,0:T(8,128)(2,1)}, bf16[512,512]{1,0:T(8,128)(2,1)}, bf16[512,128]{1,0:T(8,128)(2,1)}, bf16[512,128]{1,0:T(8,128)(2,1)}) custom-call(bf16[512,512]{1,0:T(8,128)(2,1)S(1)} %get-tuple-element.8.refs_0_, bf16[512,512]{1,0:T(8,128)(2,1)S(1)} %get-tuple-element.9.refs_1_, bf16[512,128]{1,0:T(8,128)(2,1)S(1)} %get-tuple-element.10.refs_2_, ...), custom_call_target="tpu_custom_call" | custom-call | tf_op jit(solution)/shard_map/place/pallas_call | solution.py:575
